TPU v7x, 32 devices: a whole 2x2x4 slice. The times are simulated.
32 devices in a mesh: elem: 8 (over y, x, core), mode: 4 (over z).
Axes of the slice: x: 2, y: 2, z: 4, core: 2. Of those that a mesh axis runs over, the one named last changes fastest.
Arguments:
- iterate: float32 [480, 8192], P('mode', 'elem'), may hold values from -0.75 to 0.75
- newton_residual: float32 [480, 8192], P('mode', 'elem'), may hold values from -6 to 6
- inverse_blocks: float32 [64, 8192], P(None, 'elem'), may hold values from -0.15 to 2
- basis_values: bfloat16 [1024, 480], replicated, may hold values from -4 to 4, as said below
- triple_blocks: bfloat16 [8, 60, 20160], P('mode', None, 'elem'), may hold values from -0.375 to 0.375
- block_columns: int32 [8, 4], P('mode'), may hold values from 0 to 7, as said below
- neighbour_ids: int32 [128, 6], P('elem'), may hold values from 0 to 15, as said below
Outputs:
- correction: float32 [480, 8192], P('mode', 'elem')
- linear_residual: float32 [480, 8192], P('mode', 'elem')
Inputs may be any that keep to these rules, and one draw needn't show every extreme that they name: `neighbour_ids`: columns 0 to 3 give the neighbour across the -y, +y, -z, +z faces within the element's own block of 16 elements; columns 4 and 5 the neighbour across the -x and +x faces within the previous and the next block, cyclically. Neighbours are mutual across opposite faces. `block_columns`: row b names 4 different block columns; the first is b. `basis_values`: column 0 holds ones, the constant mode.
All inputs are finite; a program needn't handle non-finite values.
Results may differ from a plain program's by a relative error of at most 0.0039.
Values may be sent and summed in bfloat16 or wider, within the bound.
A program may use at most 128 MiB of HBM per device.

v0:
```python
import math

import jax
import jax.numpy as jnp
import numpy as np
from jax import lax
from jax.sharding import PartitionSpec as P

K = 84
S = 1024
ITERS = 2
MB = 60


GROWTH = 0.5
TIME_STEP = 0.03
LIFT_SCALE = 6.0
PENALTY = 3.0
RELAX_WEIGHT = 0.8
SLAB_ENTRIES = 6291456
FACE_AXIS = (1, 1, 2, 2, 0, 0)
FACE_SIGN = (-1.0, 1.0, -1.0, 1.0, -1.0, 1.0)
FACE_OPPOSITE = (1, 0, 3, 2, 5, 4)


def padded(block, sides, width):
    for axis, dim in sides:
        count = lax.axis_size(axis)
        forward = [(i, i + 1) for i in range(count - 1)]
        forward.append((count - 1, 0))
        backward = [(target, source) for source, target in forward]
        low = lax.ppermute(
            lax.slice_in_dim(block, block.shape[dim] - width, None, axis=dim), axis, forward
        )
        high = lax.ppermute(lax.slice_in_dim(block, 0, width, axis=dim), axis, backward)
        block = jnp.concatenate([low, block, high], axis=dim)
    return block


def line_derivative():
    inward = 1.0 / math.sqrt(5.0)
    points = np.array([-1.0, -inward, inward, 1.0])
    legendre = (5.0 * points**3 - 3.0 * points) / 2.0
    matrix = np.zeros((4, 4))
    for source in range(4):
        for target in range(4):
            if source != target:
                matrix[source, target] = legendre[source] / (
                    legendre[target] * (points[source] - points[target])
                )
    matrix[0, 0] = -3.0
    matrix[3, 3] = 3.0
    return matrix


def direction_tables():
    line_matrix = line_derivative()
    identity = np.eye(4)
    singles = [
        np.kron(np.kron(line_matrix, identity), identity),
        np.kron(np.kron(identity, line_matrix), identity),
        np.kron(np.kron(identity, identity), line_matrix),
    ]
    return [np.kron(np.eye(2), single).T.astype(np.float32) for single in singles]


def face_nodes():
    layout = np.arange(64).reshape(4, 4, 4)
    return np.stack(
        [
            layout[:, 0, :].ravel(),
            layout[:, 3, :].ravel(),
            layout[:, :, 0].ravel(),
            layout[:, :, 3].ravel(),
            layout[0].ravel(),
            layout[3].ravel(),
        ]
    )


def embed_table():
    nodes_list = face_nodes()
    table_out = np.zeros((96, 64), np.float32)
    for face_index in range(6):
        for within in range(16):
            table_out[face_index * 16 + within, nodes_list[face_index, within]] = 1.0
    return table_out


def volume_derivative(field, single):
    modes_count = field.shape[0]
    paired = field.reshape(-1, 128)
    return jnp.dot(paired, single, precision=lax.Precision.HIGHEST).reshape(modes_count, -1)


def apply_inverse(field, inverse_blocks):
    modes_count = field.shape[0]
    shaped = field.reshape(modes_count, -1, 64)
    inverse = inverse_blocks.reshape(64, -1, 64)
    return jnp.einsum("mer,req->meq", shaped, inverse, precision=lax.Precision.HIGHEST).reshape(
        modes_count, -1
    )


def own_traces(values, flux_fields, face_index, axis_index):
    nodes_list = face_nodes()
    return (
        values[:, :, nodes_list[face_index]],
        flux_fields[axis_index][:, :, nodes_list[face_index]],
    )


def lift_terms(values, flux_fields, sources, near_ids, embed_matrix):
    pieces = []
    for face_index in range(6):
        own_values, own_fluxes = own_traces(values, flux_fields, face_index, FACE_AXIS[face_index])
        near_values = jnp.take(sources[face_index][0], near_ids[:, face_index], axis=1)
        near_fluxes = jnp.take(sources[face_index][1], near_ids[:, face_index], axis=1)
        pieces.append(
            LIFT_SCALE
            * (
                0.5 * FACE_SIGN[face_index] * (near_fluxes - own_fluxes)
                + PENALTY * (near_values - own_values)
            )
        )
    joined = jnp.concatenate(pieces, axis=2)
    return jnp.einsum("mef,fq->meq", joined, embed_matrix, precision=lax.Precision.HIGHEST)


def largest_divisor(number, ceiling):
    found = 1
    for candidate in range(1, ceiling + 1):
        if number % candidate == 0:
            found = candidate
    return found


def select_blocks(gathered, block_columns):
    per_row = []
    for local_row in range(block_columns.shape[0]):
        pieces_list = [
            lax.dynamic_slice_in_dim(gathered, block_columns[local_row, stored] * MB, MB, 1)
            for stored in range(block_columns.shape[1])
        ]
        per_row.append(jnp.concatenate(pieces_list, axis=1))
    return jnp.stack(per_row)


def add_slab(running, blocks_piece, selected, coeff_terms, first_row):
    row_count = blocks_piece.shape[2] // K
    ceiling_rows = max(8, SLAB_ENTRIES // (3 * K * selected.shape[0] * selected.shape[3]))
    slab_rows = largest_divisor(row_count, ceiling_rows)
    spread = coeff_terms.astype(jnp.float32)

    def one_slab(slab_index, current):
        offset = slab_index * slab_rows
        picked = lax.dynamic_slice_in_dim(selected, first_row + offset, slab_rows, 2)
        expanded = (
            picked.astype(jnp.float32)[:, :, :, None, :] * spread[None, None, None, :, :]
        ).astype(jnp.bfloat16)
        expanded = expanded.reshape(picked.shape[0], 3, slab_rows * K, picked.shape[3])
        weights = lax.dynamic_slice_in_dim(blocks_piece, offset * K, slab_rows * K, 2)
        return current + jnp.einsum(
            "bil,bcln->cbin", weights, expanded, preferred_element_type=jnp.float32
        )

    return lax.fori_loop(0, row_count // slab_rows, one_slab, running)


def apply_jacobian(
    iterate_now, coeff_terms, triple_blocks, block_columns, neighbour_ids, tables, embed_matrix
):
    modes_local, nodes_count = iterate_now.shape
    gradients = jnp.stack([volume_derivative(iterate_now, single) for single in tables]).astype(
        jnp.bfloat16
    )
    gathered = lax.all_gather(gradients, "mode", axis=1, tiled=True)
    selected = select_blocks(gathered, block_columns)
    empty_sum = jnp.zeros((3, block_columns.shape[0], MB, nodes_count), jnp.float32)
    running = add_slab(
        empty_sum,
        lax.all_gather(triple_blocks, "elem", axis=2, tiled=True),
        selected,
        coeff_terms,
        jnp.int32(0) // K,
    )
    fluxes = running.astype(jnp.bfloat16).reshape(3, modes_local, nodes_count)
    values = iterate_now.reshape(modes_local, -1, 64)
    elements = values.shape[1]
    flux_fields = fluxes.astype(jnp.float32).reshape(3, modes_local, elements, 64)
    outward = jnp.stack(
        [
            jnp.stack(own_traces(values, flux_fields, 4, 0)),
            jnp.stack(own_traces(values, flux_fields, 5, 0)),
        ]
    )
    bordered = padded(outward.reshape(2, 2, modes_local, elements * 16), (("elem", 0),), 1)
    previous_side = bordered[0].reshape(2, modes_local, elements, 16)
    next_side = bordered[3].reshape(2, modes_local, elements, 16)
    sources = [
        own_traces(values, flux_fields, FACE_OPPOSITE[face_index], FACE_AXIS[face_index])
        for face_index in range(4)
    ]
    sources = sources + [(previous_side[0], previous_side[1]), (next_side[0], next_side[1])]
    lifted = lift_terms(values, flux_fields, sources, neighbour_ids, embed_matrix)
    divergence = lifted.reshape(modes_local, -1)
    for axis_index in range(3):
        divergence = divergence + volume_derivative(
            flux_fields[axis_index].reshape(modes_local, -1), tables[axis_index]
        )
    return iterate_now - TIME_STEP * divergence


def per_device(
    iterate,
    newton_residual,
    inverse_blocks,
    basis_values,
    triple_blocks,
    block_columns,
    neighbour_ids,
):
    tables = [jnp.asarray(single) for single in direction_tables()]
    embed_matrix = jnp.asarray(embed_table())
    low_state = iterate.astype(jnp.bfloat16)
    regrouped = lax.all_to_all(low_state, "mode", split_axis=1, concat_axis=0, tiled=True)
    sampled = lax.dot_general(
        regrouped, basis_values, (((0,), (1,)), ((), ())), preferred_element_type=jnp.float32
    )
    growth = jnp.exp(GROWTH * sampled)
    leading = basis_values[:, :K].astype(jnp.float32)
    node_terms = jnp.dot(growth, leading, precision=lax.Precision.HIGHEST) / S
    coeff_terms = lax.all_gather(node_terms.T.astype(jnp.bfloat16), "mode", axis=1, tiled=True)
    correction = apply_inverse(newton_residual, inverse_blocks)
    remainder = newton_residual
    for sweep_index in range(ITERS):
        applied = apply_jacobian(
            correction,
            coeff_terms,
            triple_blocks,
            block_columns,
            neighbour_ids,
            tables,
            embed_matrix,
        )
        remainder = newton_residual - applied
        correction = correction + RELAX_WEIGHT * apply_inverse(remainder, inverse_blocks)
    return (correction, remainder)


def solution(mesh):
    return jax.shard_map(
        per_device,
        mesh=mesh,
        in_specs=(
            P("mode", "elem"),
            P("mode", "elem"),
            P(None, "elem"),
            P(),
            P("mode", None, "elem"),
            P("mode", None),
            P("elem", None),
        ),
        out_specs=(P("mode", "elem"), P("mode", "elem")),
        check_vma=False,
    )
```

profile of v0, /device:TPU:0, one launch (start us, length us, event | category | flops | bytes accessed | tf_op | source)
XLA Modules:
  0.0 2548.6 jit_solution(851366570259052936)
XLA Ops:
  90.4 57.0 %all-gather.6.cloned.1.call-done = bf16[2,60,20160]{1,0,2:T(2,128)(2,1)} async-done(((bf16[2,60,2520]{1,0,2:T(2,128)(2,1)}), bf16[2,60,20160]{1,0,2:T(2,128)(2,1)}) %all-gather.6.cloned.1.call-update) | async-done | bytes 4838416 | tf_op jit(solution)/shard_map/all_gather | solution.py:182
  169.9 1107.0 %while.32 = (s32[]{:T(128)}, f32[3,2,60,1024]{3,2,0,1:T(8,128)S(1)}, bf16[2,3,240,1024]{3,2,1,0:T(8,128)(2,1)}, f32[84,1024]{1,0:T(8,128)S(1)}, bf16[2,60,20160]...) while((s32[]{:T(128)}, ...), condition=%wide.region_1.2_spmd.clone, body=%wide.region_0.1_spmd.clone.sunk | while | flops 756375552 | bytes 119898320 | solution.py:167
  238.3 23.5 mul.610
  293.6 23.5 mul.610
  349.0 23.5 mul.610
  404.3 23.5 mul.610
  459.7 23.5 mul.610
  515.0 23.5 mul.610
  625.7 23.5 mul.610
  681.1 23.5 mul.610
  736.5 23.5 mul.610
  791.8 23.5 mul.610
  847.2 23.5 mul.610
  902.5 23.5 mul.610
  957.9 23.5 mul.610
  1013.2 23.5 mul.610
  1068.6 23.5 mul.610
  1123.9 23.5 mul.610
  1234.6 23.5 mul.610
  1338.0 48.4 %all-gather.8.cloned.1.call-done = bf16[3,480,1024]{2,1,0:T(8,128)(2,1)} async-done(((bf16[3,120,1024]{2,1,0:T(8,128)(2,1)}), bf16[3,480,1024]{2,1,0:T(8,128)(2,1)}) %all-gather.8.cloned.1.call-update) | async-done | bytes 2949136 | tf_op jit(solution)/shard_map/all_gather | solution.py:177
  1392.6 1107.2 %while.33 = (s32[]{:T(128)}, f32[3,2,60,1024]{3,2,0,1:T(8,128)S(1)}, bf16[2,3,240,1024]{3,2,1,0:T(8,128)(2,1)}, f32[84,1024]{1,0:T(8,128)S(1)}, bf16[2,60,20160]...) while((s32[]{:T(128)}, ...), condition=%wide.region_3.5_spmd.clone, body=%wide.region_2.4_spmd.clone.sunk | while | flops 756375552 | bytes 119898320 | solution.py:167
  1405.8 23.5 mul.618
  1461.2 23.5 mul.618
  1516.5 23.5 mul.618
  (640 shorter events, 1951.2 us)
Async XLA Ops:
  7.2 76.7 %all-gather.4.cloned.1.call-start = ((), (), s32[]{:S(2)}) async-start(), calls=%async_computation.1 | async-start | bytes 3686400 | tf_op jit(solution)/shard_map/all_gather | solution.py:177
  10.5 20.4 copy-start
  14.3 10.7 copy-start.102
  14.3 10.8 copy-start.77
  14.4 133.0 %all-gather.6.cloned.1.call-start = ((), (), s32[]{:S(2)}) async-start(), calls=%async_computation.2 | async-start | bytes 11612160 | tf_op jit(solution)/shard_map/all_gather | solution.py:182
  18.0 25.0 all-to-all-start
  24.3 1362.1 %all-gather.8.cloned.1.call-start = ((), (), s32[]{:S(2)}) async-start(), calls=%async_computation.3 | async-start | bytes 3686400 | tf_op jit(solution)/shard_map/all_gather | solution.py:177
  25.0 13.2 copy-start.78
  25.0 14.4 copy-start.79
  25.1 15.5 copy-start.80
  1291.7 12.1 copy-start.56
  1292.5 13.3 copy-start.20
  1292.6 13.3 copy-start.36
  1292.6 13.3 copy-start.98
  1292.6 13.4 copy-start.16
  1292.7 13.4 copy-start.35
  1292.7 13.4 copy-start.96
  1293.4 19.1 collective-permute-start
  1293.7 12.5 copy-start.18
  1293.7 12.5 copy-start.34
  1293.7 12.5 copy-start.94
  1294.4 20.6 collective-permute-start.1
  2512.4 17.8 collective-permute-start.3
  2515.0 17.8 collective-permute-start.2
  (89 other events, 381.4 us)
Sparse Core Ops, SparseCore 0:
  14.5 69.3 all-gather.3
  85.7 61.6 all-gather.5
  1326.6 59.7 all-gather.7
where the time goes:
time: 2580 us; the launch traced here: 2550 us
  local copies, waits for them, and re-layouts  1850 us (72%)
  matrix products  467 us (18%)
  waiting for transfers between devices  127 us (5%)
  other arithmetic  58.7 us (2%)
    mul x160, local copies, waits for them, and re-layouts, one_slab(): picked.astype(jnp.float32)[:, :, :, None, :]  1730 us
    dot_general x40, matrix products, one_slab(): jnp.einsum('bil,bcln->cbin', weights, expanded, preferred_element_type=jn...  444 us
    all_gather x2, waiting for transfers between devices, apply_jacobian(): gathered = lax.all_gather(gradients, 'mode', axis=1, tiled=True)  70.1 us
    all_gather x1, waiting for transfers between devices, apply_jacobian(): lax.all_gather(triple_blocks, 'elem', axis=2, tiled=True)  57 us
  transfers between devices with their start and end apart: 8, of which 3 were waited for; matrix products, arithmetic and copies ran while one was open for 3% of the time, Pallas kernels for 0%

commit v1 on v0

v1 whole, which is shorter than its diff:
```python
import functools
import math

import jax
import jax.numpy as jnp
import numpy as np
from jax import lax
from jax.experimental import pallas as pl
from jax.experimental.pallas import tpu as pltpu
from jax.sharding import PartitionSpec as P

K = 84
S = 1024
ITERS = 2
MB = 60

GROWTH = 0.5
TIME_STEP = 0.03
LIFT_SCALE = 6.0
PENALTY = 3.0
RELAX_WEIGHT = 0.8
FACE_AXIS = (1, 1, 2, 2, 0, 0)
FACE_SIGN = (-1.0, 1.0, -1.0, 1.0, -1.0, 1.0)
FACE_OPPOSITE = (1, 0, 3, 2, 5, 4)
ROWS = 64
BF = jnp.bfloat16
F32 = jnp.float32
HALF = 512
VMEM = 56 * 2**20


def line_derivative():
    inward = 1.0 / math.sqrt(5.0)
    points = np.array([-1.0, -inward, inward, 1.0])
    legendre = (5.0 * points**3 - 3.0 * points) / 2.0
    matrix = np.zeros((4, 4))
    for source in range(4):
        for target in range(4):
            if source != target:
                matrix[source, target] = legendre[source] / (
                    legendre[target] * (points[source] - points[target])
                )
    matrix[0, 0] = -3.0
    matrix[3, 3] = 3.0
    return matrix


def direction_tables():
    line_matrix = line_derivative()
    identity = np.eye(4)
    singles = [
        np.kron(np.kron(line_matrix, identity), identity),
        np.kron(np.kron(identity, line_matrix), identity),
        np.kron(np.kron(identity, identity), line_matrix),
    ]
    return [np.kron(np.eye(2), single).T for single in singles]


def face_nodes():
    layout = np.arange(64).reshape(4, 4, 4)
    return np.stack(
        [
            layout[:, 0, :].ravel(),
            layout[:, 3, :].ravel(),
            layout[:, :, 0].ravel(),
            layout[:, :, 3].ravel(),
            layout[0].ravel(),
            layout[3].ravel(),
        ]
    )


def high_low(matrix):
    matrix = jnp.asarray(matrix, F32)
    high = matrix.astype(BF)
    return high, (matrix - high.astype(F32)).astype(BF)


def gradient_table():
    return jnp.concatenate(high_low(np.concatenate(direction_tables(), axis=1)), axis=0)


def own_table():
    parts = direction_tables()
    nodes = face_nodes()
    for face in range(6):
        for pair in range(2):
            at = nodes[face] + 64 * pair
            parts[FACE_AXIS[face]][at, at] -= LIFT_SCALE * 0.5 * FACE_SIGN[face]
    return jnp.concatenate(high_low(np.concatenate(parts, axis=0)), axis=0)


def own_weight(lanes):
    counts = np.zeros(64, np.float32)
    for row in face_nodes():
        counts[row] += LIFT_SCALE * PENALTY
    return jnp.asarray(np.tile(counts, lanes // 64)[None, :])


def compaction_tables():
    nodes = face_nodes()
    out = np.zeros((6, HALF, HALF // 4), np.float32)
    for face in range(6):
        for element in range(HALF // 64):
            for within in range(16):
                out[face, element * 64 + nodes[FACE_OPPOSITE[face], within], element * 16 + within] = 1.0
    return jnp.asarray(out, BF)


def lane_ids(neighbour_ids):
    nodes = face_nodes()
    place = np.full((6, 64), -(10**6), np.int32)
    for face in range(6):
        place[face, nodes[face]] = np.arange(16)
    ids = neighbour_ids.T[:, :, None] * 16 + jnp.asarray(place)[:, None, :]
    return ids.reshape(6, -1).astype(jnp.int32)


def precondition(field, inverse, out_ref):
    rows, lanes = field.shape
    row_id = lax.broadcasted_iota(jnp.int32, (128, 128), 0) // 64
    lane_id = lax.broadcasted_iota(jnp.int32, (128, 128), 1) // 64
    same = row_id == lane_id
    for group in range(lanes // 128):
        at = slice(group * 128, group * 128 + 128)
        block = inverse[:, at]
        block = jnp.where(same, jnp.concatenate([block, block], axis=0), 0.0)
        out_ref[:, at] = jnp.dot(
            field[:, at], block, precision=lax.Precision.HIGHEST, preferred_element_type=F32
        )


def centre(field, v_ref):
    row_id = lax.broadcasted_iota(jnp.int32, (128, 128), 0) // 64
    lane_id = lax.broadcasted_iota(jnp.int32, (128, 128), 1) // 64
    average = jnp.where(row_id == lane_id, 1.0 / 64, 0.0).astype(BF)
    for group in range(field.shape[1] // 128):
        at = slice(group * 128, group * 128 + 128)
        part = field[:, at]
        mean = jnp.dot(part.astype(BF), average, preferred_element_type=F32)
        v_ref[:, at] = (part - mean).astype(BF)


def start_kernel(residual_ref, inverse_ref, w_ref, v_ref):
    precondition(residual_ref[...], inverse_ref[...], w_ref)
    centre(w_ref[...], v_ref)


def triple_kernel(chunk, columns_ref, v_ref, c_ref, t_ref, w_ref, grad_ref, pick_ref,
                  flux_ref, trace_ref, g_ref, acc_ref):
    block_rows, depth, _ = t_ref.shape
    nodes = v_ref.shape[2]
    stored = columns_ref.shape[1]
    tile = 512
    for row in range(block_rows):
        for s in range(stored):
            picked = v_ref[columns_ref[row, s]]
            at_rows = slice(s * ROWS, s * ROWS + ROWS)
            for group in range(nodes // 128):
                part = picked[:, group * 128 : group * 128 + 128]
                part = jnp.concatenate([part, part], axis=1)
                grads = jnp.dot(part, grad_ref[...], preferred_element_type=F32).astype(BF)
                for d in range(3):
                    first = d * nodes + group * 128
                    g_ref[at_rows, first : first + 128] = grads[:, d * 128 : d * 128 + 128]
        acc_ref[...] = jnp.zeros_like(acc_ref)

        def one_chunk(index, carry):
            width = chunk * ROWS
            weights = t_ref[row, :, pl.ds(pl.multiple_of(index * width, 128), width)].T
            for first in range(0, 3 * nodes, tile):
                at = slice(first, first + tile)
                product = jnp.dot(weights, g_ref[:, at], preferred_element_type=F32)
                total = acc_ref[:, at]
                node = first % nodes
                for k in range(chunk):
                    coefficient = c_ref[pl.ds(index * chunk + k, 1), node : node + tile]
                    total = total + product[k * ROWS : k * ROWS + ROWS] * coefficient
                acc_ref[:, at] = total
            return carry

        lax.fori_loop(0, K // chunk, one_chunk, 0)
        for d in range(3):
            flux_ref[d, row * ROWS : row * ROWS + ROWS, :] = acc_ref[
                :, d * nodes : d * nodes + nodes
            ].astype(BF)
    count = w_ref.shape[0]
    for face in range(6):
        mixed = LIFT_SCALE * PENALTY * w_ref[...] + (
            LIFT_SCALE * 0.5 * FACE_SIGN[face]
        ) * flux_ref[FACE_AXIS[face]].astype(F32)
        high = mixed.astype(BF)
        low = (mixed - high.astype(F32)).astype(BF)
        for half in range(nodes // HALF):
            at = slice(half * HALF, half * HALF + HALF)
            to = slice(half * HALF // 4, half * HALF // 4 + HALF // 4)
            trace_ref[face, :count, to] = jnp.dot(
                high[:, at], pick_ref[face], preferred_element_type=F32
            ).astype(BF)
            trace_ref[face, count:, to] = jnp.dot(
                low[:, at], pick_ref[face], preferred_element_type=F32
            ).astype(BF)


def finish_kernel(w_ref, residual_ref, inverse_ref, flux_ref, near_ref, before_ref, after_ref,
                  ids_ref, own_ref, weight_ref, corr_ref, lin_ref, v_ref):
    count, nodes = w_ref.shape
    for group in range(nodes // 128):
        at = slice(group * 128, group * 128 + 128)
        parts = [flux_ref[d, :, at] for d in range(3)]
        parts = jnp.concatenate(parts + parts, axis=1)
        lin_ref[:, at] = jnp.dot(parts, own_ref[...], preferred_element_type=F32)
    tile = 256
    for first in range(0, nodes, tile):
        at = slice(first, first + tile)
        total = lin_ref[:, at] - weight_ref[:, at] * w_ref[:, at]
        for face in range(6):
            if face < 4:
                trace = near_ref[face]
            else:
                trace = (before_ref if face == 4 else after_ref)[...]
            rows = lax.broadcasted_iota(jnp.int32, (trace.shape[1], tile), 0)
            spread = jnp.where(rows == ids_ref[face : face + 1, at], 1.0, 0.0).astype(BF)
            got = jnp.dot(trace, spread, preferred_element_type=F32)
            total = total + got[:count] + got[count:]
        lin_ref[:, at] = residual_ref[:, at] - (w_ref[:, at] - TIME_STEP * total)
    precondition(lin_ref[...], inverse_ref[...], corr_ref)
    corr_ref[...] = w_ref[...] + RELAX_WEIGHT * corr_ref[...]
    centre(corr_ref[...], v_ref)


VM = pl.BlockSpec(memory_space=pltpu.VMEM)
SM = pl.BlockSpec(memory_space=pltpu.SMEM)


def call(kernel, outs, ins, scratch=(), name=None):
    return pl.pallas_call(
        kernel,
        out_shape=outs,
        in_specs=ins,
        out_specs=[VM] * len(outs),
        scratch_shapes=list(scratch),
        compiler_params=pltpu.CompilerParams(vmem_limit_bytes=VMEM),
        name=name,
    )


def per_device(
    iterate,
    newton_residual,
    inverse_blocks,
    basis_values,
    triple_blocks,
    block_columns,
    neighbour_ids,
):
    modes, nodes = iterate.shape
    block_rows = triple_blocks.shape[0]
    shard = triple_blocks.shape[2] // K
    elem_count = lax.axis_size("elem")
    groups = MB // shard
    wide = ROWS // groups

    def pad_modes(field):
        field = field.reshape(modes // shard, shard, nodes)
        return jnp.pad(field, ((0, 0), (0, wide - shard), (0, 0))).reshape(-1, nodes)

    def unpad_modes(field):
        return field.reshape(modes // shard, wide, nodes)[:, :shard].reshape(modes, nodes)

    blocks = triple_blocks.reshape(block_rows, groups, shard, shard, K)
    blocks = blocks.transpose(0, 3, 4, 1, 2)
    blocks = jnp.pad(blocks, ((0, 0), (0, wide - shard), (0, 0), (0, 0), (0, wide - shard)))
    blocks = blocks.reshape(block_rows, wide, K * ROWS)
    blocks = lax.all_gather(blocks, "elem", axis=1, tiled=True)

    low_state = iterate.astype(BF)
    regrouped = lax.all_to_all(low_state, "mode", split_axis=1, concat_axis=0, tiled=True)
    sampled = jnp.dot(basis_values, regrouped, preferred_element_type=F32)
    growth = jnp.exp(GROWTH * sampled)
    leading = basis_values[:, :K]
    high = growth.astype(BF)
    low = (growth - high.astype(F32)).astype(BF)
    contract = functools.partial(
        lax.dot_general, dimension_numbers=(((0,), (0,)), ((), ())), preferred_element_type=F32
    )
    node_terms = (contract(leading, high) + contract(leading, low)) / S
    coeff_terms = lax.all_gather(node_terms.astype(BF), "mode", axis=1, tiled=True).astype(F32)

    residual = pad_modes(newton_residual)
    rows = residual.shape[0]
    field = jax.ShapeDtypeStruct((rows, nodes), F32)
    low_field = jax.ShapeDtypeStruct((rows, nodes), BF)
    ids = lane_ids(neighbour_ids)
    w, v = call(start_kernel, [field, low_field], [VM] * 2, name="start")(residual, inverse_blocks)
    forward = [(i, (i + 1) % elem_count) for i in range(elem_count)]
    backward = [(target, source) for source, target in forward]
    grads, picks, owns, weight = gradient_table(), compaction_tables(), own_table(), own_weight(nodes)
    lin = None
    for sweep in range(ITERS):
        gathered = lax.all_gather(v, "mode", axis=0, tiled=True).reshape(-1, ROWS, nodes)
        flux, traces = call(
            functools.partial(triple_kernel, 12),
            [
                jax.ShapeDtypeStruct((3, rows, nodes), BF),
                jax.ShapeDtypeStruct((6, 2 * rows, nodes // 4), BF),
            ],
            [SM] + [VM] * 6,
            [pltpu.VMEM((blocks.shape[1], 3 * nodes), BF), pltpu.VMEM((ROWS, 3 * nodes), F32)],
            name="triple",
        )(block_columns, gathered, coeff_terms, blocks, w, grads, picks)
        before = lax.ppermute(traces[4], "elem", forward)
        after = lax.ppermute(traces[5], "elem", backward)
        w, lin, v = call(finish_kernel, [field, field, low_field], [VM] * 10, name="finish")(
            w, residual, inverse_blocks, flux, traces, before, after, ids, owns, weight
        )
    return (unpad_modes(w), unpad_modes(lin))


def solution(mesh):
    return jax.shard_map(
        per_device,
        mesh=mesh,
        in_specs=(
            P("mode", "elem"),
            P("mode", "elem"),
            P(None, "elem"),
            P(),
            P("mode", None, "elem"),
            P("mode", None),
            P("elem", None),
        ),
        out_specs=(P("mode", "elem"), P("mode", "elem")),
        check_vma=False,
    )
```

time: 2580 us -> 212 us (0.08); the launches traced: 2550 us -> 211 us
  local copies, waits for them, and re-layouts: 1850 us -> 25.4 us
  matrix products: 467 us -> 3.99 us
  Pallas kernels: 0 us -> 67.1 us
  other arithmetic: 58.7 us -> 0.87 us
  waiting for transfers between devices: 127 us -> 76.5 us
    mul x162 -> x0, local copies, waits for them, and re-layouts: 1730 us -> none  [the longest x160 1730 us: one_slab(): picked.astype(jnp.float32)[:, :, :, None, :]]
    dot_general x59 -> x3, matrix products: 467 us -> 3.99 us  [the longest x2 2.31 us: per_device(): node_terms = (contract(leading, high) + contract(leading, low)) / S]
    all_gather x3, waiting for transfers between devices: 127 us -> 52.3 us  [the longest x2 27.8 us: per_device(): lax.all_gather(v, 'mode', axis=0, tiled=True).reshape(-1, ROWS, nodes)]
    pallas_call x0 -> x5, Pallas kernels: none -> 67.1 us  [the longest x2 55 us: per_device(): call(functools.partial(triple_kernel, 12), [jax.ShapeDtypeStruct((3, rows...]
    gather x72 -> x0, local copies, waits for them, and re-layouts: 42.5 us -> none  [the longest x12 13.2 us: lift_terms(): jnp.take(sources[face_index][0], near_ids[:, face_index], axis=1)]
    convert_element_type x44 -> x2, other arithmetic: 41.3 us -> 0.8 us  [the longest x1 0.77 us: per_device(): lax.all_gather(node_terms.astype(BF), 'mode', axis=1, tiled=True)]
  transfers between devices with their start and end apart: 8 -> 8, of which waited for: 3 -> 7; matrix products, arithmetic and copies ran while one was open for 3% -> 10% of each run, Pallas kernels for 0% -> 0%
where the time goes in v1:
time: 212 us; the launch traced here: 211 us
  waiting for transfers between devices  76.5 us (36%)
  Pallas kernels  67.1 us (32%)
  local copies, waits for them, and re-layouts  25.4 us (12%)
  blocking collectives  14 us (7%)
  between operations  13.8 us (7%)
  starting transfers between devices  9.53 us (4%)
  matrix products  3.99 us (2%)
    pallas_call x2, Pallas kernels, per_device(): call(functools.partial(triple_kernel, 12), [jax.ShapeDtypeStruct((3, rows...  55 us
    all_gather x2, waiting for transfers between devices, per_device(): lax.all_gather(v, 'mode', axis=0, tiled=True).reshape(-1, ROWS, nodes)  27.8 us
    all_gather x1, waiting for transfers between devices, per_device(): blocks = lax.all_gather(blocks, 'elem', axis=1, tiled=True)  24.4 us
    all_to_all x1, waiting for transfers between devices, per_device(): lax.all_to_all(low_state, 'mode', split_axis=1, concat_axis=0, tiled=True)  14.1 us
    all_gather x1, blocking collectives, per_device(): lax.all_gather(node_terms.astype(BF), 'mode', axis=1, tiled=True)  14 us
    pallas_call x2, Pallas kernels, per_device(): call(finish_kernel, [field, field, low_field], [VM] * 10, name='finish')  9.51 us
    all_to_all x1, starting transfers between devices, per_device(): lax.all_to_all(low_state, 'mode', split_axis=1, concat_axis=0, tiled=True)  6.34 us
    ppermute x2, waiting for transfers between devices, per_device(): after = lax.ppermute(traces[5], 'elem', backward)  6.29 us
  transfers between devices with their start and end apart: 8, of which 7 were waited for; matrix products, arithmetic and copies ran while one was open for 10% of the time, Pallas kernels for 0%

profile of v1, /device:TPU:0, one launch (start us, length us, event | category | flops | bytes accessed | tf_op | source)
XLA Modules:
  0.0 211.2 jit_solution(13340846201024957228)
XLA Ops:
  9.2 2.6 %start.1 = (f32[128,1024]{1,0:T(8,128)}, bf16[128,1024]{1,0:T(8,128)(2,1)}) custom-call(f32[128,1024]{1,0:T(8,128)} %bitcast.31, f32[64,1024]{1,0:T(8,128)} %inverse_ref.5), custom_call_target="tpu_custom_call" | custom-call | tf_op jit(solution)/shard_map/start/pallas_call | solution.py:295
  11.9 3.4 %reshape.47 = bf16[2,2,30,30,84]{4,3,0,2,1:T(8,128)(2,1)S(1)} reshape(bf16[2,60,2520]{2,0,1:T(2,128)(2,1)S(1)} %copy-done) | data formatting | bytes 1209600 | tf_op jit(solution)/shard_map/reshape | solution.py:271
  15.3 4.5 %copy.20 = bf16[2,30,84,2,30]{4,3,2,1,0:T(2,128)(2,1)} copy(bf16[2,30,84,2,30]{2,1,0,4,3:T(8,128)(2,1)S(1)} %bitcast.34) | data formatting | bytes 1209600
  19.9 4.5 %pad.9.clone = bf16[2,32,84,2,32]{4,3,2,1,0:T(2,128)(2,1)S(1)} pad(bf16[2,30,84,2,30]{4,3,2,1,0:T(2,128)(2,1)} %copy.20, bf16[]{:T(256)} %constant.20.clone.1), padding=0_0x0_2x0_0x0_0x0_2 | pad | bytes 1292930 | tf_op jit(solution)/shard_map/jit(_pad)/pad | solution.py:273
  24.4 2.5 %reshape.48 = bf16[2,32,5376]{2,1,0:T(8,128)(2,1)} reshape(bf16[2,32,84,2,32]{4,3,2,1,0:T(2,128)(2,1)S(1)} %pad.9.clone) | data formatting | bytes 1376256 | tf_op jit(solution)/shard_map/reshape | solution.py:274
  27.6 6.3 %all-to-all-start = ((bf16[120,4,256]{2,0,1:T(8,128)(2,1)}), bf16[120,4,256]{2,0,1:T(8,128)(2,1)S(1)}, u32[]{:S(2)}, u32[]{:S(2)}) async-start(bf16[120,4,256]{2,0,1:T(8,128)(2,1)} %bitcast.28), calls=%async_computation | async-start | bytes 491520 | tf_op jit(solution)/shard_map/all_to_all | solution.py:278
  34.0 14.1 %all-to-all-done = bf16[120,4,256]{2,0,1:T(8,128)(2,1)S(1)} async-done(((bf16[120,4,256]{2,0,1:T(8,128)(2,1)}), bf16[120,4,256]{2,0,1:T(8,128)(2,1)S(1)}, u32[]{:S(2)}, u32[]{:S(2)}) %all-to-all-start) | async-done | bytes 245792 | tf_op jit(solution)/shard_map/all_to_all | solution.py:278
  48.1 1.7 fusion
  50.9 1.2 fusion.3
  52.1 14.0 %all_gather.13 = bf16[84,1024]{1,0:T(8,128)(2,1)S(1)} all-gather(bf16[84,256]{1,0:T(8,128)(2,1)S(1)} %fusion.3), channel_id=1, replica_groups=mesh['elem'=8,'mode'=4] {'mode'}, dimensions={1}, use_global_device_ids=true | all-gather | bytes 215040 | tf_op jit(solution)/shard_map/all_gather | solution.py:288
  66.8 24.4 %all-gather.6.cloned.1.call-done.t_ref = bf16[2,256,5376]{2,1,0:T(8,128)(2,1)} async-done(((bf16[2,32,5376]{2,1,0:T(8,128)(2,1)}), bf16[2,256,5376]{2,1,0:T(8,128)(2,1)}) %all-gather.6.cloned.1.call-update) | async-done | bytes 5505040 | tf_op jit(solution)/shard_map/all_gather | solution.py:275
  91.3 27.5 %triple.2 = (bf16[3,128,1024]{2,1,0:T(8,128)(2,1)}, bf16[6,256,256]{2,1,0:T(8,128)(2,1)}) custom-call(s32[2,4]{1,0:T(2,128)} %columns_ref.3, bf16[8,64,1024]{2,1,0:T(8,128)(2,1)} %bitcast.35, f32[84,1024]{1,0:T(8,128)} %convert_element_type.49.c_ref, bf16[2,256,5376]{2,1,0:T(8,128)(2,1)} %all-gather.6.cloned.1.call-done.t_ref, ...), custom_call_target="tpu_custom_call" | custom-call | tf_op jit(solution)/shard_map/triple/pallas_call | solution.py:302
  119.7 1.4 collective-permute-start.1
  121.9 3.1 %collective-permute-done.1.after_ref = bf16[256,256]{1,0:T(8,128)(2,1)S(1)} collective-permute-done((bf16[256,256]{1,0:T(8,128)(2,1)S(1)}, bf16[256,256]{1,0:T(8,128)(2,1)S(1)}, u32[]{:S(2)}, u32[]{:S(2)}) %collective-permute-start.1) | collective-permute-done | bytes 131104 | tf_op jit(solution)/shard_map/ppermute | solution.py:313
  125.0 1.7 collective-permute-done.before_ref
  127.3 4.8 %finish.2 = (f32[128,1024]{1,0:T(8,128)}, f32[128,1024]{1,0:T(8,128)}, bf16[128,1024]{1,0:T(8,128)(2,1)}) custom-call(f32[128,1024]{1,0:T(8,128)} %get-tuple-element.12.w_ref, f32[128,1024]{1,0:T(8,128)} %bitcast.32, f32[64,1024]{1,0:T(8,128)} %inverse_ref.5, bf16[3,128,1024]{2,1,0:T(8,128)(2,1)} %get-tuple-element.14.flux_ref, ...), custom_call_target="tpu_custom_call" | custom-call | tf_op jit(solution)/shard_map/finish/pallas_call | solution.py:314
  132.1 27.8 %all-gather.8.cloned.1.call-done = bf16[512,1024]{1,0:T(8,128)(2,1)} async-done(((bf16[128,1024]{1,0:T(8,128)(2,1)}), bf16[512,1024]{1,0:T(8,128)(2,1)}) %all-gather.8.cloned.1.call-update) | async-done | bytes 1048592 | tf_op jit(solution)/shard_map/all_gather | solution.py:301
  160.0 27.5 %triple.3 = (bf16[3,128,1024]{2,1,0:T(8,128)(2,1)}, bf16[6,256,256]{2,1,0:T(8,128)(2,1)}) custom-call(s32[2,4]{1,0:T(2,128)} %columns_ref.3, bf16[8,64,1024]{2,1,0:T(8,128)(2,1)} %bitcast.36, f32[84,1024]{1,0:T(8,128)} %convert_element_type.49.c_ref, bf16[2,256,5376]{2,1,0:T(8,128)(2,1)} %all-gather.6.cloned.1.call-done.t_ref, ...), custom_call_target="tpu_custom_call" | custom-call | tf_op jit(solution)/shard_map/triple/pallas_call | solution.py:302
  188.4 1.7 collective-permute-start.3
  190.2 3.2 %collective-permute-done.3.after_ref = bf16[256,256]{1,0:T(8,128)(2,1)S(1)} collective-permute-done((bf16[256,256]{1,0:T(8,128)(2,1)S(1)}, bf16[256,256]{1,0:T(8,128)(2,1)S(1)}, u32[]{:S(2)}, u32[]{:S(2)}) %collective-permute-start.3) | collective-permute-done | bytes 131104 | tf_op jit(solution)/shard_map/ppermute | solution.py:313
  193.3 2.1 %collective-permute-done.2.before_ref = bf16[256,256]{1,0:T(8,128)(2,1)S(1)} collective-permute-done((bf16[256,256]{1,0:T(8,128)(2,1)S(1)}, bf16[256,256]{1,0:T(8,128)(2,1)S(1)}, u32[]{:S(2)}, u32[]{:S(2)}) %collective-permute-start.2) | collective-permute-done | bytes 131104 | tf_op jit(solution)/shard_map/ppermute | solution.py:312
  196.1 4.8 %finish.3 = (f32[128,1024]{1,0:T(8,128)}, f32[128,1024]{1,0:T(8,128)}, bf16[128,1024]{1,0:T(8,128)(2,1)}) custom-call(f32[128,1024]{1,0:T(8,128)} %get-tuple-element.16.w_ref, f32[128,1024]{1,0:T(8,128)} %bitcast.33, f32[64,1024]{1,0:T(8,128)} %inverse_ref.5, bf16[3,128,1024]{2,1,0:T(8,128)(2,1)} %get-tuple-element.18.flux_ref, ...), custom_call_target="tpu_custom_call" | custom-call | tf_op jit(solution)/shard_map/finish/pallas_call | solution.py:314
  200.9 1.9 reshape.51
  202.8 1.9 reshape.53
  (36 shorter events, 8.9 us)
Async XLA Ops:
  7.2 4.8 %copy-start = (bf16[2,60,2520]{2,0,1:T(2,128)(2,1)S(1)}, bf16[2,60,2520]{2,0,1:T(2,128)(2,1)}, u32[]{:S(2)}) copy-start(bf16[2,60,2520]{2,0,1:T(2,128)(2,1)} %param.16) | copy-start | bytes 1814404
  7.2 59.7 %all-gather.4.cloned.1.call-start = ((), (), s32[]{:S(2)}) async-start(), calls=%async_computation.1 | async-start | bytes 1310720 | tf_op jit(solution)/shard_map/all_gather | solution.py:301
  11.9 79.4 %all-gather.6.cloned.1.call-start = ((), (), s32[]{:S(2)}) async-start(), calls=%async_computation.2 | async-start | bytes 6193152 | tf_op jit(solution)/shard_map/all_gather | solution.py:275
  24.4 2.5 %copy-start.1 = (f32[120,1024]{1,0:T(8,128)S(1)}, f32[120,1024]{1,0:T(8,128)}, u32[]{:S(2)}) copy-start(f32[120,1024]{1,0:T(8,128)} %param.12) | copy-start | bytes 1474564
  24.4 9.6 %copy-start.7 = (s32[16,6]{0,1:T(8,128)S(1)}, s32[16,6]{0,1:T(8,128)}, u32[]{:S(2)}) copy-start(s32[16,6]{0,1:T(8,128)} %param.18) | copy-start | bytes 1156
  27.6 20.5 %all-to-all-start = ((bf16[120,4,256]{2,0,1:T(8,128)(2,1)}), bf16[120,4,256]{2,0,1:T(8,128)(2,1)S(1)}, u32[]{:S(2)}, u32[]{:S(2)}) async-start(bf16[120,4,256]{2,0,1:T(8,128)(2,1)} %bitcast.28), calls=%async_computation | async-start | bytes 491520 | tf_op jit(solution)/shard_map/all_to_all | solution.py:278
  34.0 126.0 %all-gather.8.cloned.1.call-start = ((), (), s32[]{:S(2)}) async-start(), calls=%async_computation.3 | async-start | bytes 1310720 | tf_op jit(solution)/shard_map/all_gather | solution.py:301
  91.3 29.9 %copy-start.6 = (s32[6,64]{1,0:T(8,128)S(1)}, s32[6,64]{1,0:T(8,128)}, u32[]{:S(2)}) copy-start(s32[6,64]{1,0:T(8,128)} %constant.22.clone) | copy-start | bytes 4612
  119.7 5.3 %collective-permute-start.1 = (bf16[256,256]{1,0:T(8,128)(2,1)S(1)}, bf16[256,256]{1,0:T(8,128)(2,1)S(1)}, u32[]{:S(2)}, u32[]{:S(2)}) collective-permute-start(bf16[256,256]{1,0:T(8,128)(2,1)S(1)} %get-tuple-element.24), channel_id=1, source_target_pairs={{4,0},{8,4},{12,8},{16,12},{20,16},{24,20},{28,24},{0,28},{5,1},{9... | collective-permute-start | bytes 393224 | tf_op jit(solution)/shard_map/ppermute | solution.py:313
  121.1 5.6 %collective-permute-start = (bf16[256,256]{1,0:T(8,128)(2,1)S(1)}, bf16[256,256]{1,0:T(8,128)(2,1)S(1)}, u32[]{:S(2)}, u32[]{:S(2)}) collective-permute-start(bf16[256,256]{1,0:T(8,128)(2,1)S(1)} %get-tuple-element.25), channel_id=1, source_target_pairs={{0,4},{4,8},{8,12},{12,16},{16,20},{20,24},{24,28},{28,0},{1,5},{5... | collective-permute-start | bytes 393224 | tf_op jit(solution)/shard_map/ppermute | solution.py:312
  125.0 1.7 copy-start.2
  126.7 0.6 copy-start.4
  188.4 4.9 %collective-permute-start.3 = (bf16[256,256]{1,0:T(8,128)(2,1)S(1)}, bf16[256,256]{1,0:T(8,128)(2,1)S(1)}, u32[]{:S(2)}, u32[]{:S(2)}) collective-permute-start(bf16[256,256]{1,0:T(8,128)(2,1)S(1)} %get-tuple-element.22), channel_id=1, source_target_pairs={{4,0},{8,4},{12,8},{16,12},{20,16},{24,20},{28,24},{0,28},{5,1},{9... | collective-permute-start | bytes 393224 | tf_op jit(solution)/shard_map/ppermute | solution.py:313
  190.2 5.3 %collective-permute-start.2 = (bf16[256,256]{1,0:T(8,128)(2,1)S(1)}, bf16[256,256]{1,0:T(8,128)(2,1)S(1)}, u32[]{:S(2)}, u32[]{:S(2)}) collective-permute-start(bf16[256,256]{1,0:T(8,128)(2,1)S(1)} %get-tuple-element.23), channel_id=1, source_target_pairs={{0,4},{4,8},{8,12},{12,16},{16,20},{20,24},{24,28},{28,0},{1,5},{5... | collective-permute-start | bytes 393224 | tf_op jit(solution)/shard_map/ppermute | solution.py:312
  193.3 2.1 %copy-start.3 = (bf16[256,256]{1,0:T(8,128)(2,1)}, bf16[256,256]{1,0:T(8,128)(2,1)S(1)}, u32[]{:S(2)}) copy-start(bf16[256,256]{1,0:T(8,128)(2,1)S(1)} %collective-permute-done.3.after_ref) | copy-start | bytes 393220
  195.5 0.7 copy-start.5
Sparse Core Ops, SparseCore 0:
  12.0 36.3 all-gather.3
  50.3 40.9 all-gather.5
  132.2 27.6 all-gather.7

commit v2 on v1

--- a/solution.py
+++ b/solution.py
@@ -141,14 +141,86 @@
         v_ref[:, at] = (part - mean).astype(BF)
 
 
-def start_kernel(residual_ref, inverse_ref, w_ref, v_ref):
+MESH = pl.DeviceIdType.MESH
+
+
+def greet(devices):
+    barrier = pltpu.get_barrier_semaphore()
+    for device in devices:
+        pl.semaphore_signal(barrier, inc=1, device_id=device, device_id_type=MESH)
+    pl.semaphore_wait(barrier, len(devices))
+
+
+def push(source, target, send, receive, device):
+    copy = pltpu.make_async_remote_copy(
+        src_ref=source,
+        dst_ref=target,
+        send_sem=send,
+        recv_sem=receive,
+        device_id=device,
+        device_id_type=MESH,
+    )
+    copy.start()
+    return copy
+
+
+def start_kernel(mode_count, elem_count, t_ref, low_ref, basis_ref, leading_ref, residual_ref,
+                 inverse_ref, t_all, v_all, c_all, w_ref, low_all, growth_ref,
+                 own_sem, t_sem, mate_sem, low_sem, v_sem, c_sem):
+    m, e = lax.axis_index("mode"), lax.axis_index("elem")
+    pairs = elem_count // 2
+    mate = (e + 1 - 2 * lax.rem(e, 2), m)
+    across = [None] + [(lax.rem(e + 2 * k, elem_count), m) for k in range(1, pairs)]
+    along = [None] + [(e, lax.rem(m + k, mode_count)) for k in range(1, mode_count)]
+    greet([mate] + across[1:] + along[1:])
+    copies = []
+    for k in range(1, mode_count):
+        copies.append(
+            push(low_ref.at[along[k][1]], low_all.at[m], low_sem.at[0, k], low_sem.at[1, k], along[k])
+        )
+    lows = list(copies)
+    blocks = [
+        push(t_ref, t_all.at[e], t_sem.at[0, k], t_sem.at[1, k], across[k]) for k in range(1, pairs)
+    ]
+    mates = [push(t_ref, t_all.at[e], mate_sem.at[0, 0], mate_sem.at[1, 0], mate)]
+    own = pltpu.make_async_copy(t_ref, t_all.at[e], own_sem)
+    own.start()
+    low_all[m] = low_ref[m]
     precondition(residual_ref[...], inverse_ref[...], w_ref)
-    centre(w_ref[...], v_ref)
+    centre(w_ref[...], v_all.at[m])
+    fields = [
+        push(v_all.at[m], v_all.at[m], v_sem.at[0, k], v_sem.at[1, k], along[k])
+        for k in range(1, mode_count)
+    ]
+    for copy in lows:
+        copy.wait_recv()
+    state = low_all[...].reshape(-1, low_all.shape[2])
+    sampled = jnp.dot(basis_ref[...], state, preferred_element_type=F32)
+    growth_ref[...] = jnp.exp(GROWTH * sampled)
+    high = growth_ref[...].astype(BF)
+    low = (growth_ref[...] - high.astype(F32)).astype(BF)
+    terms = jnp.dot(leading_ref[...], high, preferred_element_type=F32)
+    terms = terms + jnp.dot(leading_ref[...], low, preferred_element_type=F32)
+    c_all[m] = (terms / S).astype(BF)
+    terms_out = [
+        push(c_all.at[m], c_all.at[m], c_sem.at[0, k], c_sem.at[1, k], along[k])
+        for k in range(1, mode_count)
+    ]
+    for k in range(1, pairs):
+        blocks[k - 1].wait_recv()
+        got = lax.rem(e + elem_count - 2 * k, elem_count)
+        mates.append(push(t_all.at[got], t_all.at[got], mate_sem.at[0, k], mate_sem.at[1, k], mate))
+    for copy in lows + blocks:
+        copy.wait_send()
+    for copy in fields + terms_out + mates:
+        copy.wait()
+    own.wait()
 
 
 def triple_kernel(chunk, columns_ref, v_ref, c_ref, t_ref, w_ref, grad_ref, pick_ref,
                   flux_ref, trace_ref, g_ref, acc_ref):
-    block_rows, depth, _ = t_ref.shape
+    shards, block_rows, wide, _ = t_ref.shape
+    depth = shards * wide
     nodes = v_ref.shape[2]
     stored = columns_ref.shape[1]
     tile = 512
@@ -167,7 +239,8 @@
 
         def one_chunk(index, carry):
             width = chunk * ROWS
-            weights = t_ref[row, :, pl.ds(pl.multiple_of(index * width, 128), width)].T
+            weights = t_ref[:, row, :, pl.ds(pl.multiple_of(index * width, 128), width)]
+            weights = weights.reshape(depth, width).T
             for first in range(0, 3 * nodes, tile):
                 at = slice(first, first + tile)
                 product = jnp.dot(weights, g_ref[:, at], preferred_element_type=F32)
@@ -202,45 +275,78 @@
             ).astype(BF)
 
 
-def finish_kernel(w_ref, residual_ref, inverse_ref, flux_ref, near_ref, before_ref, after_ref,
-                  ids_ref, own_ref, weight_ref, corr_ref, lin_ref, v_ref):
+def finish_kernel(mode_count, elem_count, last, w_ref, residual_ref, inverse_ref, flux_ref, near_ref,
+                  ids_ref, own_ref, weight_ref, *refs):
+    if last:
+        corr_ref, lin_ref, side_ref, side_sem = refs
+        v_all, v_sem = None, None
+    else:
+        corr_ref, lin_ref, v_all, side_ref, side_sem, v_sem = refs
     count, nodes = w_ref.shape
+    m, e = lax.axis_index("mode"), lax.axis_index("elem")
+    after = (lax.rem(e + 1, elem_count), m)
+    before = (lax.rem(e + elem_count - 1, elem_count), m)
+    along = [(e, lax.rem(m + k, mode_count)) for k in range(1, mode_count)]
+    greet([before, after] + ([] if last else along))
+    sides = [
+        push(near_ref.at[4], side_ref.at[0], side_sem.at[0, 0], side_sem.at[1, 0], after),
+        push(near_ref.at[5], side_ref.at[1], side_sem.at[0, 1], side_sem.at[1, 1], before),
+    ]
     for group in range(nodes // 128):
         at = slice(group * 128, group * 128 + 128)
         parts = [flux_ref[d, :, at] for d in range(3)]
         parts = jnp.concatenate(parts + parts, axis=1)
         lin_ref[:, at] = jnp.dot(parts, own_ref[...], preferred_element_type=F32)
     tile = 256
-    for first in range(0, nodes, tile):
-        at = slice(first, first + tile)
-        total = lin_ref[:, at] - weight_ref[:, at] * w_ref[:, at]
-        for face in range(6):
-            if face < 4:
-                trace = near_ref[face]
-            else:
-                trace = (before_ref if face == 4 else after_ref)[...]
+
+    def spread_faces(total, traces, faces, at):
+        for trace, face in zip(traces, faces):
             rows = lax.broadcasted_iota(jnp.int32, (trace.shape[1], tile), 0)
             spread = jnp.where(rows == ids_ref[face : face + 1, at], 1.0, 0.0).astype(BF)
             got = jnp.dot(trace, spread, preferred_element_type=F32)
             total = total + got[:count] + got[count:]
+        return total
+
+    for first in range(0, nodes, tile):
+        at = slice(first, first + tile)
+        total = lin_ref[:, at] - weight_ref[:, at] * w_ref[:, at]
+        lin_ref[:, at] = spread_faces(total, [near_ref[f] for f in range(4)], range(4), at)
+    for copy in sides:
+        copy.wait()
+    sent = []
+    for index, first in enumerate(range(0, nodes, tile)):
+        at = slice(first, first + tile)
+        total = spread_faces(lin_ref[:, at], [side_ref[0], side_ref[1]], (4, 5), at)
         lin_ref[:, at] = residual_ref[:, at] - (w_ref[:, at] - TIME_STEP * total)
-    precondition(lin_ref[...], inverse_ref[...], corr_ref)
-    corr_ref[...] = w_ref[...] + RELAX_WEIGHT * corr_ref[...]
-    centre(corr_ref[...], v_ref)
+        precondition(lin_ref[:, at], inverse_ref[:, at], corr_ref.at[:, pl.ds(first, tile)])
+        corr_ref[:, at] = w_ref[:, at] + RELAX_WEIGHT * corr_ref[:, at]
+        if not last:
+            part = v_all.at[m, :, pl.ds(first, tile)]
+            centre(corr_ref[:, at], part)
+            for k in range(1, mode_count):
+                sent.append(
+                    push(part, part, v_sem.at[0, index, k], v_sem.at[1, index, k], along[k - 1])
+                )
+    for copy in sent:
+        copy.wait()
 
 
 VM = pl.BlockSpec(memory_space=pltpu.VMEM)
 SM = pl.BlockSpec(memory_space=pltpu.SMEM)
 
 
-def call(kernel, outs, ins, scratch=(), name=None):
+AN = pl.BlockSpec(memory_space=pl.ANY)
+
+
+def call(kernel, outs, ins, scratch=(), name=None, out_specs=None, remote=None):
+    more = {} if remote is None else {"collective_id": remote, "has_side_effects": True}
     return pl.pallas_call(
         kernel,
         out_shape=outs,
         in_specs=ins,
-        out_specs=[VM] * len(outs),
+        out_specs=out_specs or [VM] * len(outs),
         scratch_shapes=list(scratch),
-        compiler_params=pltpu.CompilerParams(vmem_limit_bytes=VMEM),
+        compiler_params=pltpu.CompilerParams(vmem_limit_bytes=VMEM, **more),
         name=name,
     )
 
@@ -272,33 +378,51 @@
     blocks = blocks.transpose(0, 3, 4, 1, 2)
     blocks = jnp.pad(blocks, ((0, 0), (0, wide - shard), (0, 0), (0, 0), (0, wide - shard)))
     blocks = blocks.reshape(block_rows, wide, K * ROWS)
-    blocks = lax.all_gather(blocks, "elem", axis=1, tiled=True)
-
-    low_state = iterate.astype(BF)
-    regrouped = lax.all_to_all(low_state, "mode", split_axis=1, concat_axis=0, tiled=True)
-    sampled = jnp.dot(basis_values, regrouped, preferred_element_type=F32)
-    growth = jnp.exp(GROWTH * sampled)
-    leading = basis_values[:, :K]
-    high = growth.astype(BF)
-    low = (growth - high.astype(F32)).astype(BF)
-    contract = functools.partial(
-        lax.dot_general, dimension_numbers=(((0,), (0,)), ((), ())), preferred_element_type=F32
-    )
-    node_terms = (contract(leading, high) + contract(leading, low)) / S
-    coeff_terms = lax.all_gather(node_terms.astype(BF), "mode", axis=1, tiled=True).astype(F32)
+
+    mode_count = lax.axis_size("mode")
+    share = nodes // mode_count
+    low_state = pad_modes(iterate.astype(BF))
+    rows = low_state.shape[0]
+    low_state = low_state.reshape(rows, mode_count, share).transpose(1, 0, 2)
+    basis = jnp.pad(
+        basis_values.reshape(S, -1, shard), ((0, 0), (0, 0), (0, wide - shard))
+    ).reshape(S, -1)
+    terms_rows = -(-K // 16) * 16
+    leading = jnp.pad(basis_values[:, :K].T, ((0, terms_rows - K), (0, 0)))
 
     residual = pad_modes(newton_residual)
-    rows = residual.shape[0]
     field = jax.ShapeDtypeStruct((rows, nodes), F32)
-    low_field = jax.ShapeDtypeStruct((rows, nodes), BF)
+    all_fields = jax.ShapeDtypeStruct((mode_count, rows, nodes), BF)
     ids = lane_ids(neighbour_ids)
-    w, v = call(start_kernel, [field, low_field], [VM] * 2, name="start")(residual, inverse_blocks)
-    forward = [(i, (i + 1) % elem_count) for i in range(elem_count)]
-    backward = [(target, source) for source, target in forward]
     grads, picks, owns, weight = gradient_table(), compaction_tables(), own_table(), own_weight(nodes)
+    dma = pltpu.SemaphoreType.DMA
+    blocks, v, terms, w = call(
+        functools.partial(start_kernel, mode_count, elem_count),
+        [
+            jax.ShapeDtypeStruct((elem_count,) + blocks.shape, BF),
+            all_fields,
+            jax.ShapeDtypeStruct((mode_count, terms_rows, share), BF),
+            field,
+        ],
+        [AN] + [VM] * 5,
+        [
+            pltpu.VMEM((mode_count, rows, share), BF),
+            pltpu.VMEM((S, share), F32),
+            dma,
+            dma((2, elem_count // 2)),
+            dma((2, elem_count // 2)),
+            dma((2, mode_count)),
+            dma((2, mode_count)),
+            dma((2, mode_count)),
+        ],
+        name="start",
+        out_specs=[AN, VM, VM, VM],
+        remote=0,
+    )(blocks, low_state, basis, leading, residual, inverse_blocks)
+    coeff_terms = terms.transpose(1, 0, 2).reshape(terms_rows, nodes).astype(F32)
     lin = None
     for sweep in range(ITERS):
-        gathered = lax.all_gather(v, "mode", axis=0, tiled=True).reshape(-1, ROWS, nodes)
+        last = sweep == ITERS - 1
         flux, traces = call(
             functools.partial(triple_kernel, 12),
             [
@@ -306,14 +430,20 @@
                 jax.ShapeDtypeStruct((6, 2 * rows, nodes // 4), BF),
             ],
             [SM] + [VM] * 6,
-            [pltpu.VMEM((blocks.shape[1], 3 * nodes), BF), pltpu.VMEM((ROWS, 3 * nodes), F32)],
+            [pltpu.VMEM((elem_count * wide, 3 * nodes), BF), pltpu.VMEM((ROWS, 3 * nodes), F32)],
             name="triple",
-        )(block_columns, gathered, coeff_terms, blocks, w, grads, picks)
-        before = lax.ppermute(traces[4], "elem", forward)
-        after = lax.ppermute(traces[5], "elem", backward)
-        w, lin, v = call(finish_kernel, [field, field, low_field], [VM] * 10, name="finish")(
-            w, residual, inverse_blocks, flux, traces, before, after, ids, owns, weight
-        )
+        )(block_columns, v.reshape(-1, ROWS, nodes), coeff_terms, blocks, w, grads, picks)
+        results = call(
+            functools.partial(finish_kernel, mode_count, elem_count, last),
+            [field, field] + ([] if last else [all_fields]),
+            [VM] * 8,
+            [pltpu.VMEM((2, 2 * rows, nodes // 4), BF), dma((2, 2))]
+            + ([] if last else [dma((2, nodes // 256, mode_count))]),
+            name="finish",
+            remote=2 if last else 1,
+        )(w, residual, inverse_blocks, flux, traces, ids, owns, weight)
+        w, lin = results[:2]
+        v = None if last else results[2]
     return (unpad_modes(w), unpad_modes(lin))
 
 

time: 212 us -> 173 us (0.82)
  waiting for transfers between devices: 76.5 us -> 0 us
  Pallas kernels: 67.1 us -> 143 us
  blocking collectives: 14 us -> 0 us
  between operations: 13.8 us -> 0.76 us
  starting transfers between devices: 9.53 us -> 0 us
  matrix products: 3.99 us -> 0 us
  other arithmetic: 0.87 us -> 3.52 us
    pallas_call x3, Pallas kernels: 12.1 us -> 87.5 us  [the longest x2 44.4 us: per_device(): call(functools.partial(finish_kernel, mode_count, elem_count, last), [fie...]
    all_gather x3 -> x0, waiting for transfers between devices: 52.3 us -> none  [the longest x2 27.8 us: per_device(): lax.all_gather(v, 'mode', axis=0, tiled=True).reshape(-1, ROWS, nodes)]
    all_to_all x1 -> x0, waiting for transfers between devices: 14.1 us -> none  [per_device(): lax.all_to_all(low_state, 'mode', split_axis=1, concat_axis=0, tiled=True)]
    all_gather x1 -> x0, blocking collectives: 14 us -> none  [per_device(): lax.all_gather(node_terms.astype(BF), 'mode', axis=1, tiled=True)]
    ppermute x4 -> x0, waiting for transfers between devices: 10.1 us -> none  [the longest x2 6.29 us: per_device(): after = lax.ppermute(traces[5], 'elem', backward)]
    all_to_all x1 -> x0, starting transfers between devices: 6.34 us -> none  [per_device(): lax.all_to_all(low_state, 'mode', split_axis=1, concat_axis=0, tiled=True)]
    dot_general x3 -> x0, matrix products: 3.99 us -> none  [the longest x2 2.31 us: per_device(): node_terms = (contract(leading, high) + contract(leading, low)) / S]
    ppermute x4 -> x0, starting transfers between devices: 3.11 us -> none  [the longest x2 3.11 us: per_device(): after = lax.ppermute(traces[5], 'elem', backward)]
  transfers between devices with their start and end apart: 8 -> 0, of which waited for: 7 -> 0; matrix products, arithmetic and copies ran while one was open for 10% -> 0% of each run, Pallas kernels for 0% -> 0%
where the time goes in v2:
time: 173 us
  Pallas kernels  143 us (83%)
  local copies, waits for them, and re-layouts  25.6 us (15%)
  other arithmetic  3.52 us (2%)
    pallas_call x2, Pallas kernels, per_device(): call(functools.partial(triple_kernel, 12), [jax.ShapeDtypeStruct((3, rows...  55.4 us
    pallas_call x2, Pallas kernels, per_device(): call(functools.partial(finish_kernel, mode_count, elem_count, last), [fie...  44.4 us
    pallas_call x1, Pallas kernels, per_device(): call(functools.partial(start_kernel, mode_count, elem_count), [jax.ShapeD...  43.1 us
    unnamed x7, local copies, waits for them, and re-layouts  4.5 us
    pad x1, local copies, waits for them, and re-layouts, per_device(): jnp.pad(blocks, ((0, 0), (0, wide - shard), (0, 0), (0, 0), (0, wide - sh...  4.46 us
    reshape x2, local copies, waits for them, and re-layouts, unpad_modes(): field.reshape(modes // shard, wide, nodes)[:, :shard].reshape(modes, nodes)  3.75 us

profile of v2, /device:TPU:0, one launch (start us, length us, event | category | flops | bytes accessed | tf_op | source)
XLA Modules:
  0.0 172.7 jit_solution(14327311456005441467)
XLA Ops:
  0.6 0.7 multiply_bitcast_fusion
  1.4 0.8 broadcast_add_fusion
  2.2 0.7 add.30.ids_ref
  2.8 1.0 slice_bitcast_fusion
  3.8 0.7 pad.23.leading_ref
  4.5 1.1 convert_element_type.38
  5.7 0.2 reshape_reshape.3
  5.9 0.7 copy.24
  6.7 0.8 pad.24
  7.5 3.4 %reshape.53 = bf16[2,2,30,30,84]{4,3,0,2,1:T(8,128)(2,1)S(1)} reshape(bf16[2,60,2520]{2,0,1:T(2,128)(2,1)S(1)} %copy-done.1) | data formatting | bytes 1209600 | tf_op jit(solution)/shard_map/reshape | solution.py:377
  10.9 0.3 reshape.56
  11.3 1.5 copy.19.basis_ref
  12.9 4.5 %copy.21 = bf16[2,30,84,2,30]{4,3,2,1,0:T(2,128)(2,1)} copy(bf16[2,30,84,2,30]{2,1,0,4,3:T(8,128)(2,1)S(1)} %bitcast.28) | data formatting | bytes 1209600
  17.4 4.5 %pad.20.clone = bf16[2,32,84,2,32]{4,3,2,1,0:T(2,128)(2,1)S(1)} pad(bf16[2,30,84,2,30]{4,3,2,1,0:T(2,128)(2,1)} %copy.21, bf16[]{:T(256)} %constant.14.clone.1), padding=0_0x0_2x0_0x0_0x0_2 | pad | bytes 1292930 | tf_op jit(solution)/shard_map/jit(_pad)/pad | solution.py:379
  21.8 2.5 %reshape.54.t_ref = bf16[2,32,5376]{2,1,0:T(8,128)(2,1)} reshape(bf16[2,32,84,2,32]{4,3,2,1,0:T(2,128)(2,1)S(1)} %pad.20.clone) | data formatting | bytes 1376256 | tf_op jit(solution)/shard_map/reshape | solution.py:380
  24.3 43.1 %start.1 = (bf16[8,2,32,5376]{3,2,1,0:T(8,128)(2,1)}, bf16[4,128,1024]{2,1,0:T(8,128)(2,1)}, bf16[4,96,256]{2,1,0:T(8,128)(2,1)}, f32[128,1024]{1,0:T(8,128)}) custom-call(bf16[2,32,5376]{2,1,0:T(8,128)(2,1)} %reshape.54.t_ref, bf16[4,128,256]{2,1,0:T(8,128)(2,1)} %bitcast.33, bf16[1024,512]{1,0:T(8,128)(2,1)} %copy.19.basis_ref, ...), custom_call_target="tpu_custom_call" | custom-call | tf_op jit(solution)/shard_map/start/pallas_call | solution.py:399
  67.4 1.0 convert_bitcast_fusion
  68.4 0.8 copy.22
  69.1 27.7 %triple.2 = (bf16[3,128,1024]{2,1,0:T(8,128)(2,1)}, bf16[6,256,256]{2,1,0:T(8,128)(2,1)}) custom-call(s32[2,4]{1,0:T(2,128)} %columns_ref.3, bf16[8,64,1024]{2,1,0:T(8,128)(2,1)} %bitcast.31, f32[96,1024]{1,0:T(8,128)} %bitcast.29, bf16[8,2,32,5376]{3,2,1,0:T(8,128)(2,1)} %get-tuple-element.17.t_ref, f32[128,1024]{1,0:T(8,128)} %get-tuple-element.14.w_ref, ...), custom_call_target="tpu_custom_call" | custom-call | tf_op jit(solution)/shard_map/triple/pallas_call | solution.py:426
  96.8 33.4 %finish.2 = (f32[128,1024]{1,0:T(8,128)}, f32[128,1024]{1,0:T(8,128)}, bf16[4,128,1024]{2,1,0:T(8,128)(2,1)}) custom-call(f32[128,1024]{1,0:T(8,128)} %get-tuple-element.14.w_ref, f32[128,1024]{1,0:T(8,128)} %bitcast.25, f32[64,1024]{1,0:T(8,128)} %inverse_ref.5, bf16[3,128,1024]{2,1,0:T(8,128)(2,1)} %get-tuple-element.18.flux_ref, ...), custom_call_target="tpu_custom_call" | custom-call | tf_op jit(solution)/shard_map/finish/pallas_call | solution.py:436
  130.2 27.7 %triple.3 = (bf16[3,128,1024]{2,1,0:T(8,128)(2,1)}, bf16[6,256,256]{2,1,0:T(8,128)(2,1)}) custom-call(s32[2,4]{1,0:T(2,128)} %columns_ref.3, bf16[8,64,1024]{2,1,0:T(8,128)(2,1)} %bitcast.32, f32[96,1024]{1,0:T(8,128)} %bitcast.30, bf16[8,2,32,5376]{3,2,1,0:T(8,128)(2,1)} %get-tuple-element.17.t_ref, f32[128,1024]{1,0:T(8,128)} %get-tuple-element.20.w_ref, ...), custom_call_target="tpu_custom_call" | custom-call | tf_op jit(solution)/shard_map/triple/pallas_call | solution.py:426
  157.9 11.0 %finish.3 = (f32[128,1024]{1,0:T(8,128)}, f32[128,1024]{1,0:T(8,128)}) custom-call(f32[128,1024]{1,0:T(8,128)} %get-tuple-element.20.w_ref, f32[128,1024]{1,0:T(8,128)} %bitcast.26, f32[64,1024]{1,0:T(8,128)} %inverse_ref.5, bf16[3,128,1024]{2,1,0:T(8,128)(2,1)} %get-tuple-element.22.flux_ref, bf16[6,256,256]{2,1,0:T(8,128)(2,1)} %get-tuple-element.23.near_ref, ...), custom_call_target="tpu_custom_call" | custom-call | tf_op jit(solution)/shard_map/finish/pallas_call | solution.py:436
  168.9 1.9 %reshape.63 = f32[120,1024]{1,0:T(8,128)} reshape(f32[4,30,1024]{2,1,0:T(8,128)} %bitcast.35) | data formatting | bytes 983040 | tf_op jit(solution)/shard_map/reshape | solution.py:375
  170.8 1.9 %reshape.65 = f32[120,1024]{1,0:T(8,128)} reshape(f32[4,30,1024]{2,1,0:T(8,128)} %bitcast.34) | data formatting | bytes 983040 | tf_op jit(solution)/shard_map/reshape | solution.py:375
  (10 shorter events, 0.3 us)
Async XLA Ops:
  0.6 6.0 %copy-start.2 = (f32[120,1024]{1,0:T(8,128)S(1)}, f32[120,1024]{1,0:T(8,128)}, u32[]{:S(2)}) copy-start(f32[120,1024]{1,0:T(8,128)} %param.13) | copy-start | bytes 1474564
  2.8 4.7 %copy-start.1 = (bf16[2,60,2520]{2,0,1:T(2,128)(2,1)S(1)}, bf16[2,60,2520]{2,0,1:T(2,128)(2,1)}, u32[]{:S(2)}) copy-start(bf16[2,60,2520]{2,0,1:T(2,128)(2,1)} %param.16) | copy-start | bytes 1814404
  5.6 5.3 %copy-start = (bf16[1024,480]{0,1:T(8,128)(2,1)S(1)}, bf16[1024,480]{0,1:T(8,128)(2,1)}, u32[]{:S(2)}) copy-start(bf16[1024,480]{0,1:T(8,128)(2,1)} %param.15) | copy-start | bytes 2949124
